TPU v7x, 32 devices: a whole 2x2x4 slice. The times are simulated.
32 devices in a mesh: row: 4 (over y, x), col: 8 (over z, core).
Axes of the slice: x: 2, y: 2, z: 4, core: 2. Of those that a mesh axis runs over, the one named last changes fastest.
Arguments:
- forcing: float32 [2, 8, 16, 16384], P(None, None, None, ('row', 'col')), may hold values from -6 to 6
- elem_area: float32 [16384], P(('row', 'col')), may hold values from 0.5 to 2
- send_elem: int32 [4, 64, 128], P('row', 'col'), may hold values from -1 to 511, as said below
- intersection_entry_slot: int32 [4, 8192], P(None, ('row', 'col')), may hold values from -1 to 1023, as said below
- entry_weight: float32 [4, 8192], P(None, ('row', 'col')), may hold values from 0.1 to 1
- entry_coords: float32 [2, 4, 8192], P(None, None, ('row', 'col')), may hold values from -1 to 1
- land_area: float32 [8192], P(('row', 'col')), may hold values from 1 to 4
- soil_temp: float32 [20, 8192], P(None, ('row', 'col')), may hold values from 0.5 to 1.5
- soil_cond: float32 [20, 8192], P(None, ('row', 'col')), may hold values from 0.2 to 2
- heat_cap: float32 [20, 8192], P(None, ('row', 'col')), may hold values from 0.5 to 2
- layer_count: int32 [8192], P(('row', 'col')), may hold values from 8 to 20
- snow_count: int32 [8192], P(('row', 'col')), may hold values from 0 to 5
- mix: float32 [8], replicated, may hold values from 0.3 to 1
Outputs:
- flux_nodes: float32 [2, 4, 16, 16384], P(None, None, None, ('row', 'col'))
- soil_new: float32 [20, 8192], P(None, ('row', 'col'))
Inputs may be any that keep to these rules, and one draw needn't show every extreme that they name: `send_elem`: -1 marks an empty slot. Intersections are local: block o of device c goes to device (c - o + 4) mod 8 of the same row. In each block of 128 slots the filled slots come first, 32 or more are filled, and every device fills one block completely. `intersection_entry_slot`: -1 marks an unused entry. A value q names slot q % 128 of block q // 128 that device (p + q // 128 - 8 // 2) mod 8 of the same row sends to this device p; every filled slot sent to a device is read by exactly one of its entries, unfilled ones by none; the first entry of every cell is used.
All inputs are finite; a program needn't handle non-finite values.
Results may differ from a plain program's by a relative error of at most 0.0015.
Values may be sent and summed in bfloat16 or wider, within the bound.
A program may use at most 64 MiB of HBM per device.

v0:
```python
import functools

import jax
import jax.numpy as jnp
import numpy as np
from jax import lax
from jax.experimental import pallas as pl
from jax.experimental.pallas import tpu as pltpu
from jax.sharding import PartitionSpec as P

MODES = 6
SUB = 2
FIELDS = 4
ROWS = SUB * FIELDS
NODES = 16
LOAD_ORDER = (0, 12, 13, 2, 3, 4, 5, 7, 8, 9, 10, 11, 1, 6, 14)
MESH = pl.DeviceIdType.MESH
F32 = jnp.float32
BF16 = jnp.bfloat16


def legendre(degree, position):
    if degree == 0:
        return 1.0 + 0.0 * position
    if degree == 1:
        return position
    return 1.5 * position * position - 0.5


def modal_tables():
    points = np.array([-1.0, -1.0 / np.sqrt(5.0), 1.0 / np.sqrt(5.0), 1.0])
    weights = np.array([1.0 / 6.0, 5.0 / 6.0, 5.0 / 6.0, 1.0 / 6.0])
    pairs = [(0, 0), (1, 0), (0, 1), (2, 0), (1, 1), (0, 2)]
    project = np.zeros((MODES, NODES))
    basis = np.zeros((NODES, MODES))
    for a in range(4):
        for b in range(4):
            for m, (i, j) in enumerate(pairs):
                value = legendre(i, points[a]) * legendre(j, points[b])
                basis[4 * a + b, m] = value
                scale = (2 * i + 1) * (2 * j + 1) / 4.0
                project[m, 4 * a + b] = weights[a] * weights[b] * scale * value
    return project, basis


def split_table(table):
    table = table.astype(np.float32)
    high = table.astype(BF16)
    low = (table - high.astype(np.float32)).astype(BF16)
    return jnp.asarray(np.concatenate([high, high, low], axis=1).astype(np.float32))


def block_tables():
    project, basis = modal_tables()
    wide_project = np.zeros((MODES * ROWS, ROWS * NODES))
    wide_basis = np.zeros((ROWS * NODES, MODES * ROWS))
    for m in range(MODES):
        for r in range(ROWS):
            wide_project[m * ROWS + r, r * NODES : (r + 1) * NODES] = project[m]
            wide_basis[r * NODES : (r + 1) * NODES, m * ROWS + r] = basis[:, m]
    return split_table(wide_project), split_table(wide_basis)


def split(values):
    high = values.astype(BF16)
    low = (values - high.astype(F32)).astype(BF16)
    return high, low


def dot(a, b):
    return jnp.dot(a, b, preferred_element_type=F32)


def dot_t(a, b):
    return lax.dot_general(a, b, (((1,), (1,)), ((), ())), preferred_element_type=F32)


def one_hot(mask):
    return jnp.where(mask, 1.0, 0.0).astype(BF16)


def weighted_basis(weight, u, v):
    return [
        weight,
        weight * u,
        weight * v,
        weight * (1.5 * u * u - 0.5),
        weight * (u * v),
        weight * (1.5 * v * v - 0.5),
    ]


def kernel(
    nrows,
    ncols,
    span,
    cap,
    stages,
    *refs,
):
    operands, (out_ref, soil_ref), refs = refs[:15], refs[15:17], refs[17:]
    held, refs = refs[:15], refs[15:]
    (
    coef_send,
    coef_recv,
    point_send,
    point_recv,
    flux_send,
    flux_recv,
    total_send,
    total_recv,
    elem_hot,
    slot_hot,
    coef_sems,
    point_sems,
    flux_sems,
    total_sems,
        load_sems,
    ) = refs
    (
        forcing_ref,
        area_ref,
        send_ref,
        slot_ref,
        weight_ref,
        coords_ref,
        land_area_ref,
        temp_ref,
        cond_ref,
        heat_ref,
        layers_ref,
        snow_ref,
        mix_ref,
        project_ref,
        basis_ref,
    ) = held
    loads = [
        pltpu.make_async_copy(operands[i], held[i], load_sems.at[i]) for i in range(15)
    ]
    for i in LOAD_ORDER:
        loads[i].start()
    row, col = lax.axis_index("row"), lax.axis_index("col")
    half = span // 2
    elems = forcing_ref.shape[3]
    entries, cells = slot_ref.shape
    layers = temp_ref.shape[0]

    def device(dr, dc):
        return (lax.rem(row + dr % nrows, nrows), lax.rem(col + dc % ncols, ncols))

    offsets = {(0, d % ncols) for d in range(-half, half + 1)}
    for stage in stages:
        offsets |= set(stage)
    offsets = sorted(offsets - {(0, 0)})
    barrier = pltpu.get_barrier_semaphore()
    for dr, dc in offsets:
        pl.semaphore_signal(barrier, inc=1, device_id=device(dr, dc), device_id_type=MESH)

    for i in (0, 12, 13, 2):
        loads[i].wait()

    rows = []
    for s in range(SUB):
        mixed = (0.5 * mix_ref[0]) * forcing_ref[s, 0]
        for f in range(1, forcing_ref.shape[1]):
            mixed = mixed + (0.5 * mix_ref[f]) * forcing_ref[s, f]
        rows += [mixed, forcing_ref[s, 2], forcing_ref[s, 3], forcing_ref[s, 4]]
    high, low = split(jnp.concatenate(rows, axis=0))
    coef = dot(project_ref[...].astype(BF16), jnp.concatenate([high, low, high], axis=0)).astype(BF16)

    elem_iota = lax.broadcasted_iota(jnp.int32, (elems, cap), 0)
    for o in range(span):
        elem_hot[:, o * cap : (o + 1) * cap] = one_hot(elem_iota == send_ref[o : o + 1, :])
    sent = dot(coef, elem_hot[...]).astype(BF16)
    for o in range(span):
        coef_send[o] = sent[:, o * cap : (o + 1) * cap]

    pl.semaphore_wait(barrier, len(offsets))

    def exchange(source, target, sems, direction):
        copies = {}
        for o in range(span):
            if o == half:
                continue
            copies[o] = pltpu.make_async_remote_copy(
                src_ref=source.at[o],
                dst_ref=target.at[o],
                send_sem=sems.at[0, o],
                recv_sem=sems.at[1, o],
                device_id=device(0, direction * (half - o)),
                device_id_type=MESH,
            )
            copies[o].start()
        return copies

    coef_copies = exchange(coef_send, coef_recv, coef_sems, 1)

    for i in (3, 4, 5):
        loads[i].wait()

    q = slot_ref[...]
    weight = jnp.where(q >= 0, weight_ref[...], 0.0)
    weight_sum = jnp.sum(weight, axis=0, keepdims=True)
    share = weight / weight_sum

    def flat(values):
        return jnp.concatenate([values[k : k + 1, :] for k in range(entries)], axis=1)

    qf = flat(q)
    stacked = jnp.concatenate(
        [flat(coords_ref[0]), flat(coords_ref[1]), flat(weight), flat(share)], axis=0
    )
    stacked_high = stacked.astype(BF16).astype(F32)
    stacked = jnp.concatenate([stacked_high, stacked - stacked_high], axis=0)
    place_hot = one_hot(
        lax.broadcasted_iota(jnp.int32, (cap, entries * cells), 0) == (qf & (cap - 1))
    )
    by_block = jnp.concatenate(
        [
            jnp.where((qf >= o * cap) & (qf < (o + 1) * cap), stacked, 0.0)
            for o in range(span)
        ],
        axis=0,
    ).astype(BF16)
    points = dot_t(by_block, place_hot)
    for o in range(span):
        point_send[o] = points[o * 8 : (o + 1) * 8]
    point_copies = exchange(point_send, point_recv, point_sems, -1)

    place_iota = lax.broadcasted_iota(jnp.int32, (cap, cells), 0)
    for o in range(span):
        here = place_iota == q[0:1, :] - o * cap
        for k in range(1, entries):
            here = here | (place_iota == q[k : k + 1, :] - o * cap)
        slot_hot[o * cap : (o + 1) * cap, :] = one_hot(here)

    def lanes(blocks):
        return jnp.concatenate(blocks, axis=1)

    def slot_points(tiles):
        wide = lanes(tiles)
        wide = wide[0:4] + wide[4:8]
        return wide[0:1], wide[1:2], wide[2:3], wide[3:4]

    u, v, _, share_slot = slot_points([points[o * 8 : (o + 1) * 8] for o in range(span)])
    land_basis = weighted_basis(share_slot, u, v)

    for i in (7, 8, 9, 10, 11, 1, 6, 14):
        loads[i].wait()
    layer_count, snow_count = layers_ref[...], snow_ref[...]
    heat = [heat_ref[z : z + 1, :] for z in range(layers)]
    start = [temp_ref[z : z + 1, :] for z in range(layers)]
    conduct = [
        jnp.where(z < snow_count, 0.25, 1.0) * cond_ref[z : z + 1, :] for z in range(layers)
    ]
    link = [
        jnp.where(
            z + 1 < layer_count,
            2.0 * conduct[z] * conduct[z + 1] / (conduct[z] + conduct[z + 1]),
            0.0,
        )
        for z in range(layers - 1)
    ]
    inverse, ratio, shift = [None] * layers, [None] * layers, [None] * layers
    for z in reversed(range(1, layers)):
        pivot = heat[z] + link[z - 1]
        right = heat[z] * start[z]
        if z + 1 < layers:
            pivot = pivot + link[z] * (1.0 - ratio[z + 1])
            right = right + link[z] * shift[z + 1]
        inverse[z] = 1.0 / pivot
        ratio[z] = link[z - 1] * inverse[z]
        shift[z] = right * inverse[z]
    base, gain = [jnp.zeros_like(heat[0])], [jnp.ones_like(heat[0])]
    for z in range(1, layers):
        base.append(shift[z] + ratio[z] * base[z - 1])
        gain.append(ratio[z] * gain[z - 1])
    shift_base, shift_gain = [None] * layers, [None] * layers
    for z in reversed(range(1, layers)):
        right_base, right_gain = heat[z] * base[z], heat[z] * gain[z]
        if z + 1 < layers:
            right_base = right_base + link[z] * shift_base[z + 1]
            right_gain = right_gain + link[z] * shift_gain[z + 1]
        shift_base[z] = right_base * inverse[z]
        shift_gain[z] = right_gain * inverse[z]
    top_pivot = heat[0] + link[0] * (1.0 - ratio[1])

    for o in coef_copies:
        coef_copies[o].wait_recv()
    got = [(coef_send if o == half else coef_recv)[o].astype(F32) for o in range(span)]
    at_points = jnp.zeros((ROWS, span * cap), F32)
    for m in range(MODES):
        at_points = at_points + land_basis[m] * lanes(
            [block[m * ROWS : (m + 1) * ROWS] for block in got]
        )
    high, low = split(at_points)
    gathered = dot(jnp.concatenate([high, low], axis=0), slot_hot[...])
    land = gathered[0:ROWS] + gathered[ROWS : 2 * ROWS]

    flux = []
    tops = []
    for s in range(SUB):
        absorbed, t_air, passed, driver = (
            land[s * FIELDS + i : s * FIELDS + i + 1] for i in range(FIELDS)
        )
        exch = 0.5 + 0.5 * driver * driver
        if s == 0:
            before, below = start[0], shift[1]
        else:
            before, below = tops[0], shift_base[1] + shift_gain[1] * tops[0]
        top = (heat[0] * before + absorbed + exch * t_air + link[0] * below) / (
            top_pivot + exch
        )
        second = below + ratio[1] * top
        tops.append(top)
        flux += [exch * (top - t_air), top, link[0] * (top - second), exch * passed]
    flux = jnp.concatenate(flux, axis=0)
    high, low = split(flux)
    spread = dot_t(jnp.concatenate([high, low], axis=0), slot_hot[...])
    spread = spread[0:ROWS] + spread[ROWS : 2 * ROWS]
    for o in range(span):
        flux_send[o] = spread[:, o * cap : (o + 1) * cap]
    flux_copies = exchange(flux_send, flux_recv, flux_sems, -1)

    excess = land_area_ref[...] - weight_sum
    partial = jnp.sum(excess * flux, axis=1, keepdims=True)
    lane = lax.broadcasted_iota(jnp.int32, (ROWS, cap), 1)
    place = lax.broadcasted_iota(jnp.int32, (ROWS, cap), 0)
    total = jnp.sum(jnp.where(lane == place, partial, 0.0), axis=0, keepdims=True)
    area = area_ref[...]
    area_total = jnp.sum(area, axis=1, keepdims=True)
    total = total + jnp.where(lane[0:1] == ROWS, area_total, 0.0)
    total_copies = []
    first = 0

    def send_total(stage, first, total):
        total_send[first] = total
        copies = []
        for i, (dr, dc) in enumerate(stage):
            copy = pltpu.make_async_remote_copy(
                src_ref=total_send.at[first],
                dst_ref=total_recv.at[first + i],
                send_sem=total_sems.at[0, first + i],
                recv_sem=total_sems.at[1, first + i],
                device_id=device(dr, dc),
                device_id_type=MESH,
            )
            copy.start()
            copies.append(copy)
        return copies

    def sum_total(stage, first, total, copies):
        for copy in copies:
            copy.wait_recv()
        for i in range(len(stage)):
            total = total + total_recv[first + i]
        return total

    pending = send_total(stages[0], 0, total)
    total_copies += pending

    rest, slope = jnp.zeros_like(heat[0]), jnp.zeros_like(heat[0])
    soil_ref[0:1, :] = tops[1]
    for z in range(1, layers):
        rest = shift_base[z] + ratio[z] * rest
        slope = shift_gain[z] + ratio[z] * slope
        soil_ref[z : z + 1, :] = rest + slope * tops[0] + gain[z] * tops[1]

    for o in point_copies:
        point_copies[o].wait_recv()
    u, v, weight_slot, _ = slot_points(
        [(point_send if o == half else point_recv)[o] for o in range(span)]
    )
    elem_basis = weighted_basis(weight_slot, u, v)
    for o in flux_copies:
        flux_copies[o].wait_recv()
    back = lanes([(flux_send if o == half else flux_recv)[o] for o in range(span)])
    terms = jnp.concatenate([elem_basis[m] * back for m in range(MODES)], axis=0)
    high, low = split(terms)
    summed = dot_t(jnp.concatenate([high, low], axis=0), elem_hot[...])
    count = MODES * ROWS
    element_coef = (summed[0:count] + summed[count : 2 * count]) / area
    high, low = split(element_coef)
    nodes = dot(basis_ref[...].astype(BF16), jnp.concatenate([high, low, high], axis=0))

    total = sum_total(stages[0], 0, total, pending)
    first = len(stages[0])
    for stage in stages[1:]:
        pending = send_total(stage, first, total)
        total_copies += pending
        total = sum_total(stage, first, total, pending)
        first += len(stage)
    spread_total = jnp.broadcast_to(total, (ROWS, cap))
    budget = jnp.sum(jnp.where(lane == place, spread_total, 0.0), axis=1, keepdims=True)
    all_area = jnp.sum(jnp.where(lane == ROWS, spread_total, 0.0), axis=1, keepdims=True)
    correction = budget / all_area
    for r in range(ROWS):
        out_ref[r // FIELDS, r % FIELDS] = (
            nodes[r * NODES : (r + 1) * NODES] + correction[r : r + 1, :]
        )

    for copies in (coef_copies, point_copies, flux_copies):
        for o in copies:
            copies[o].wait_send()
    for copy in total_copies:
        copy.wait_send()


def local(nrows, ncols, *args):
    (
        forcing,
        elem_area,
        send_elem,
        slots,
        entry_weight,
        entry_coords,
        land_area,
        soil_temp,
        soil_cond,
        heat_cap,
        layer_count,
        snow_count,
        mix,
    ) = args
    _, span, cap = send_elem.shape
    elems = forcing.shape[3]
    cells = land_area.shape[0]
    if nrows * ncols <= 64:
        stages = [
            [(r, c) for r in range(nrows) for c in range(ncols) if (r, c) != (0, 0)]
        ]
    else:
        stages = [[(r, 0) for r in range(1, nrows)], [(0, c) for c in range(1, ncols)]]
    peers = sum(len(stage) for stage in stages)
    project, basis = block_tables()
    vmem = pl.BlockSpec(memory_space=pltpu.VMEM)
    hbm = pl.BlockSpec(memory_space=pltpu.HBM)
    operands = (
        forcing,
        elem_area.reshape(1, elems),
        send_elem.reshape(span, cap),
        slots,
        entry_weight,
        entry_coords,
        land_area.reshape(1, cells),
        soil_temp,
        soil_cond,
        heat_cap,
        layer_count.reshape(1, cells),
        snow_count.reshape(1, cells),
        mix,
        project,
        basis,
    )
    held = [
        (pltpu.SMEM if i == 12 else pltpu.VMEM)(x.shape, x.dtype)
        for i, x in enumerate(operands)
    ]
    return pl.pallas_call(
        functools.partial(kernel, nrows, ncols, span, cap, stages),
        out_shape=(
            jax.ShapeDtypeStruct((SUB, FIELDS, NODES, elems), F32),
            jax.ShapeDtypeStruct(soil_temp.shape, F32),
        ),
        in_specs=[hbm] * 15,
        out_specs=(vmem, vmem),
        scratch_shapes=held
        + [
            pltpu.VMEM((span, MODES * ROWS, cap), BF16),
            pltpu.VMEM((span, MODES * ROWS, cap), BF16),
            pltpu.VMEM((span, 8, cap), F32),
            pltpu.VMEM((span, 8, cap), F32),
            pltpu.VMEM((span, ROWS, cap), F32),
            pltpu.VMEM((span, ROWS, cap), F32),
            pltpu.VMEM((peers, 1, cap), F32),
            pltpu.VMEM((peers, 1, cap), F32),
            pltpu.VMEM((elems, span * cap), BF16),
            pltpu.VMEM((span * cap, cells), BF16),
            pltpu.SemaphoreType.DMA((2, span)),
            pltpu.SemaphoreType.DMA((2, span)),
            pltpu.SemaphoreType.DMA((2, span)),
            pltpu.SemaphoreType.DMA((2, peers)),
            pltpu.SemaphoreType.DMA((15,)),
        ],
        compiler_params=pltpu.CompilerParams(
            collective_id=0, has_side_effects=True, vmem_limit_bytes=60 * 1024 * 1024
        ),
    )(*operands)


def solution(mesh):
    placed = (
        P(None, None, None, ("row", "col")),
        P(("row", "col")),
        P("row", "col", None),
        P(None, ("row", "col")),
        P(None, ("row", "col")),
        P(None, None, ("row", "col")),
        P(("row", "col")),
        P(None, ("row", "col")),
        P(None, ("row", "col")),
        P(None, ("row", "col")),
        P(("row", "col")),
        P(("row", "col")),
        P(),
    )
    return jax.shard_map(
        functools.partial(local, mesh.shape["row"], mesh.shape["col"]),
        mesh=mesh,
        in_specs=placed,
        out_specs=(P(None, None, None, ("row", "col")), P(None, ("row", "col"))),
        check_vma=False,
    )
```

profile of v0, /device:TPU:0, one launch (start us, length us, event | category | flops | bytes accessed | tf_op | source)
XLA Modules:
  0.0 21.5 jit_solution(14143455768014935857)
XLA Ops:
  0.6 18.6 %shard_map.158 = (f32[2,4,16,512]{3,2,1,0:T(8,128)}, f32[20,256]{1,0:T(8,128)}) custom-call(f32[2,8,16,512]{3,2,1,0:T(8,128)} %refs_0_.1, f32[1,512]{1,0:T(1,128)} %bitcast.6, s32[8,128]{1,0:T(8,128)} %bitcast.5, s32[4,256]{1,0:T(4,128)} %refs_3_.1, f32[4,256]{1,0:T(4,128)} %refs_4_.1, f32[2,4,256]{2,1,0:T(4,128)} %refs_5_.1, f32[1,256]{1,0:T(1,128)} %bitcast.7, ...), custom_call_target="tpu_custom_call" | custom-call | tf_op jit(solution)/shard_map/pallas_call | solution.py:459
  19.3 0.0 copy-start
  19.3 1.7 %copy.19 = f32[2,4,16,512]{3,2,1,0:T(8,128)} copy(f32[2,4,16,512]{3,2,1,0:T(8,128)} %get-tuple-element.4) | data formatting | bytes 524288
  20.9 0.0 copy-done
  20.9 0.6 %copy.20 = f32[20,256]{1,0:T(8,128)} copy(f32[20,256]{1,0:T(8,128)S(1)} %copy-done) | data formatting | bytes 40960
Async XLA Ops:
  19.3 1.7 %copy-start = (f32[20,256]{1,0:T(8,128)S(1)}, f32[20,256]{1,0:T(8,128)}, u32[]{:S(2)}) copy-start(f32[20,256]{1,0:T(8,128)} %get-tuple-element.5) | copy-start | bytes 61444
where the time goes:
time: 21.7 us; the launch traced here: 21.5 us
  Pallas kernels  18.6 us (86%)
  local copies, waits for them, and re-layouts  2.29 us (11%)
  between operations  0.65 us (3%)
    pallas_call x1, Pallas kernels, local(): pl.pallas_call(functools.partial(kernel, nrows, ncols, span, cap, stages)...  18.6 us
    unnamed x4, local copies, waits for them, and re-layouts  2.29 us

commit v1 on v0

--- a/solution.py
+++ b/solution.py
@@ -404,6 +404,26 @@
             copies[o].wait_send()
     for copy in total_copies:
         copy.wait_send()
+
+
+def pass_on(nodes_ref, soil_ref, out_ref, soil_out_ref, nodes_held, soil_held, sems):
+    steps = [(soil_ref, soil_held, soil_out_ref)]
+    for r in range(ROWS):
+        at = (r // FIELDS, r % FIELDS)
+        steps.append((nodes_ref.at[at], nodes_held.at[at], out_ref.at[at]))
+    reads = [
+        pltpu.make_async_copy(a, b, sems.at[0, i]) for i, (a, b, _) in enumerate(steps)
+    ]
+    writes = [
+        pltpu.make_async_copy(b, c, sems.at[1, i]) for i, (_, b, c) in enumerate(steps)
+    ]
+    for read in reads:
+        read.start()
+    for read, write in zip(reads, writes):
+        read.wait()
+        write.start()
+    for write in writes:
+        write.wait()
 
 
 def local(nrows, ncols, *args):
@@ -456,7 +476,7 @@
         (pltpu.SMEM if i == 12 else pltpu.VMEM)(x.shape, x.dtype)
         for i, x in enumerate(operands)
     ]
-    return pl.pallas_call(
+    nodes, soil = pl.pallas_call(
         functools.partial(kernel, nrows, ncols, span, cap, stages),
         out_shape=(
             jax.ShapeDtypeStruct((SUB, FIELDS, NODES, elems), F32),
@@ -486,6 +506,21 @@
             collective_id=0, has_side_effects=True, vmem_limit_bytes=60 * 1024 * 1024
         ),
     )(*operands)
+    return pl.pallas_call(
+        pass_on,
+        out_shape=(
+            jax.ShapeDtypeStruct(nodes.shape, F32),
+            jax.ShapeDtypeStruct(soil.shape, F32),
+        ),
+        in_specs=[hbm] * 2,
+        out_specs=(hbm, hbm),
+        scratch_shapes=[
+            pltpu.VMEM(nodes.shape, F32),
+            pltpu.VMEM(soil.shape, F32),
+            pltpu.SemaphoreType.DMA((2, ROWS + 1)),
+        ],
+        compiler_params=pltpu.CompilerParams(vmem_limit_bytes=60 * 1024 * 1024),
+    )(nodes, soil)
 
 
 def solution(mesh):

time: 21.7 us -> 21.1 us (0.972)
  local copies, waits for them, and re-layouts: 2.29 us -> 0 us
  Pallas kernels: 18.6 us -> 20.3 us
    unnamed x4 -> x0, local copies, waits for them, and re-layouts: 2.29 us -> none
    pallas_call x0 -> x1, Pallas kernels: none -> 1.66 us  [local(): pl.pallas_call(pass_on, out_shape=(jax.ShapeDtypeStruct(nodes.shape, F32)...]
where the time goes in v1:
time: 21.1 us; the launch traced here: 20.9 us
  Pallas kernels  20.3 us (96%)
  between operations  0.64 us (3%)
    pallas_call x1, Pallas kernels, local(): pl.pallas_call(functools.partial(kernel, nrows, ncols, span, cap, stages)...  18.6 us
    pallas_call x1, Pallas kernels, local(): pl.pallas_call(pass_on, out_shape=(jax.ShapeDtypeStruct(nodes.shape, F32)...  1.66 us

profile of v1, /device:TPU:0, one launch (start us, length us, event | category | flops | bytes accessed | tf_op | source)
XLA Modules:
  0.0 20.9 jit_solution(14619525702515815125)
XLA Ops:
  0.6 18.6 %shard_map.158 = (f32[2,4,16,512]{3,2,1,0:T(8,128)}, f32[20,256]{1,0:T(8,128)}) custom-call(f32[2,8,16,512]{3,2,1,0:T(8,128)} %refs_0_.1, f32[1,512]{1,0:T(1,128)} %bitcast.6, s32[8,128]{1,0:T(8,128)} %bitcast.5, s32[4,256]{1,0:T(4,128)} %refs_3_.1, f32[4,256]{1,0:T(4,128)} %refs_4_.1, f32[2,4,256]{2,1,0:T(4,128)} %refs_5_.1, f32[1,256]{1,0:T(1,128)} %bitcast.7, ...), custom_call_target="tpu_custom_call" | custom-call | tf_op jit(solution)/shard_map/pallas_call | solution.py:479
  19.3 1.7 %shard_map.159 = (f32[2,4,16,512]{3,2,1,0:T(8,128)}, f32[20,256]{1,0:T(8,128)}) custom-call(f32[2,4,16,512]{3,2,1,0:T(8,128)} %get-tuple-element.4.nodes_ref, f32[20,256]{1,0:T(8,128)} %get-tuple-element.5.soil_ref), custom_call_target="tpu_custom_call" | custom-call | tf_op jit(solution)/shard_map/pallas_call | solution.py:509
